TPU v7x, 32 devices: a whole 2x2x4 slice. The times are simulated.
32 devices in a mesh: dp: 16 (over z, y, x), tensor: 2 (over core).
Axes of the slice: x: 2, y: 2, z: 4, core: 2. Of those that a mesh axis runs over, the one named last changes fastest.
Arguments:
- tokens: bfloat16 [16, 1024, 1024], P('dp'), may hold values from -6 to 6
- cotangent: bfloat16 [16, 1024, 1024], P('dp'), may hold values from -6 to 6
- lengths: int32 [16], P('dp'), may hold values from 128 to 1024, as said below
- noise_times: int32 [16], P('dp'), may hold values from 0 to 255
- query_weight: bfloat16 [1024, 1024], P(None, 'tensor'), may hold values from -0.1875 to 0.1875
- key_weight: bfloat16 [1024, 1024], P(None, 'tensor'), may hold values from -0.1875 to 0.1875
- value_weight: bfloat16 [1024, 1024], P(None, 'tensor'), may hold values from -0.1875 to 0.1875
- merge_weight: bfloat16 [1024, 1024], P('tensor'), may hold values from -0.75 to 0.75
- up_weight: bfloat16 [1024, 4096], P(None, 'tensor'), may hold values from -0.1875 to 0.1875
- down_weight: bfloat16 [4096, 1024], P('tensor'), may hold values from -0.09375 to 0.09375
- first_scales: float32 [256, 1024], replicated, may hold values from 0.1 to 1.9
- second_scales: float32 [256, 1024], replicated, may hold values from 0.1 to 1.9
Outputs:
- layer_output: bfloat16 [16, 1024, 1024], P('dp')
- grad_tokens: bfloat16 [16, 1024, 1024], P('dp')
- grad_query: float32 [1024, 1024], P('dp', 'tensor')
- grad_key: float32 [1024, 1024], P('dp', 'tensor')
- grad_value: float32 [1024, 1024], P('dp', 'tensor')
- grad_merge: float32 [1024, 1024], P('tensor', 'dp')
- grad_up: float32 [1024, 4096], P('dp', 'tensor')
- grad_down: float32 [4096, 1024], P('tensor', 'dp')
- grad_first: float32 [256, 1024], P(None, 'dp')
- grad_second: float32 [256, 1024], P(None, 'dp')
Inputs may be any that keep to these rules, and one draw needn't show every extreme that they name: `lengths`: some sequence has exactly 1024 tokens; the others have at least 128.
All inputs are finite; a program needn't handle non-finite values.
Results may differ from a plain program's by a relative error of at most 0.014.
Values sent between devices are 32-bit elements; how exact they have to be, the bound alone decides.
A program may use at most 192 MiB of HBM per device.

v0:
```python
import math

import jax
import jax.numpy as jnp
from jax import lax
from jax.sharding import PartitionSpec as P

HEAD = 64


epsilon = 1e-05
highest = lax.Precision.HIGHEST


def gelu_tanh(values):
    return (
        0.5
        * values
        * (1.0 + jnp.tanh(0.7978845608028654 * (values + 0.044715 * values * values * values)))
    )


def rope_tables(length, head_size):
    halves = head_size // 2
    places = jnp.arange(length, dtype=jnp.float32)[:, None]
    frequency = jnp.exp(
        jnp.arange(halves, dtype=jnp.float32) * (-2.0 * math.log(10000.0) / head_size)
    )
    angles = places * frequency[None, :]
    return (jnp.cos(angles), jnp.sin(angles))


def rotate(values, cos_table, sin_table):
    halves = values.shape[-1] // 2
    first_half = values[..., :halves]
    second_half = values[..., halves:]
    cosine = cos_table[:, None, :]
    sine_part = sin_table[:, None, :]
    return jnp.concatenate(
        [
            first_half * cosine - second_half * sine_part,
            second_half * cosine + first_half * sine_part,
        ],
        axis=-1,
    )


def unrotate(gradient, cos_table, sin_table):
    halves = gradient.shape[-1] // 2
    first_half = gradient[..., :halves]
    second_half = gradient[..., halves:]
    cosine = cos_table[:, None, :]
    sine_part = sin_table[:, None, :]
    return jnp.concatenate(
        [
            first_half * cosine + second_half * sine_part,
            second_half * cosine - first_half * sine_part,
        ],
        axis=-1,
    )


def normalize(values):
    centred = values - jnp.mean(values, axis=-1, keepdims=True)
    inv_std = lax.rsqrt(jnp.mean(centred * centred, axis=-1, keepdims=True) + epsilon)
    return (centred * inv_std, inv_std)


def norm_back(grad_norm, normed, inv_std, scale_rows):
    grad_hat = grad_norm * scale_rows[:, None, :]
    grad_scale = jnp.sum(grad_norm * normed, axis=1)
    mean_grad = jnp.mean(grad_hat, axis=-1, keepdims=True)
    mean_cross = jnp.mean(grad_hat * normed, axis=-1, keepdims=True)
    return (inv_std * (grad_hat - mean_grad - normed * mean_cross), grad_scale)


def block_scores(query_block, key_rot, key_bias, scale_factor):
    scores = jnp.einsum("sqhd,skhd->shqk", query_block, key_rot, preferred_element_type=jnp.float32)
    return scores * scale_factor + key_bias[:, None, None, :]


def body(
    tokens,
    cotangent,
    lengths,
    noise_times,
    query_weight,
    key_weight,
    value_weight,
    merge_weight,
    up_weight,
    down_weight,
    first_scales,
    second_scales,
):
    seq_count, length, width = tokens.shape
    local_width = query_weight.shape[1]
    local_heads = local_width // HEAD
    table_rows = first_scales.shape[0]
    flat_rows = seq_count * length
    scale_factor = 1.0 / math.sqrt(HEAD)
    block_rows = min(512, length)
    head_shape = (seq_count, length, local_heads, HEAD)
    row_mask = (jnp.arange(length, dtype=jnp.int32)[None, :] < lengths[:, None]).astype(jnp.float32)
    key_bias = (row_mask - 1.0) * 1000000000.0
    one_hot = (noise_times[:, None] == jnp.arange(table_rows, dtype=jnp.int32)[None, :]).astype(
        jnp.float32
    )
    scale_one = jnp.dot(one_hot, first_scales, precision=highest)
    scale_two = jnp.dot(one_hot, second_scales, precision=highest)
    cos_table, sin_table = rope_tables(length, HEAD)
    inputs = tokens.astype(jnp.float32) * row_mask[:, :, None]
    normed_one, inv_one = normalize(inputs)
    normal_in = (normed_one * scale_one[:, None, :]).astype(jnp.bfloat16).reshape(flat_rows, width)
    queries = jnp.dot(normal_in, query_weight, preferred_element_type=jnp.float32).reshape(
        head_shape
    )
    key_proj = jnp.dot(normal_in, key_weight, preferred_element_type=jnp.float32).reshape(
        head_shape
    )
    value_rows = (
        jnp.dot(normal_in, value_weight, preferred_element_type=jnp.float32)
        .astype(jnp.bfloat16)
        .reshape(head_shape)
    )
    query_rot = rotate(queries, cos_table, sin_table).astype(jnp.bfloat16)
    key_rot = rotate(key_proj, cos_table, sin_table).astype(jnp.bfloat16)
    attended = []
    log_sums = []
    for offset in range(0, length, block_rows):
        scores = block_scores(
            query_rot[:, offset : offset + block_rows], key_rot, key_bias, scale_factor
        )
        peak_score = jnp.max(scores, axis=-1, keepdims=True)
        exponent = jnp.exp(scores - peak_score)
        totals = jnp.sum(exponent, axis=-1, keepdims=True)
        soft_weights = (exponent / totals).astype(jnp.bfloat16)
        log_sums.append(peak_score + jnp.log(totals))
        attended.append(
            jnp.einsum(
                "shqk,skhd->sqhd", soft_weights, value_rows, preferred_element_type=jnp.float32
            )
        )
    heads_out = (
        jnp.concatenate(attended, axis=1).astype(jnp.bfloat16).reshape(flat_rows, local_width)
    )
    attn_part = jnp.dot(heads_out, merge_weight, preferred_element_type=jnp.float32)
    attn_total = lax.psum(attn_part, "tensor")
    hidden_one = inputs + attn_total.reshape(seq_count, length, width)
    normed_two, inv_two = normalize(hidden_one)
    normal_mid = (normed_two * scale_two[:, None, :]).astype(jnp.bfloat16).reshape(flat_rows, width)
    pre_act = jnp.dot(normal_mid, up_weight, preferred_element_type=jnp.float32)
    activated = gelu_tanh(pre_act).astype(jnp.bfloat16)
    mlp_part = jnp.dot(activated, down_weight, preferred_element_type=jnp.float32)
    mlp_total = lax.psum(mlp_part, "tensor")
    layer_output = (
        (hidden_one + mlp_total.reshape(seq_count, length, width)) * row_mask[:, :, None]
    ).astype(jnp.bfloat16)
    grad_final = cotangent.astype(jnp.float32) * row_mask[:, :, None]
    grad_mlp = grad_final.astype(jnp.bfloat16).reshape(flat_rows, width)
    grad_down = jnp.dot(activated.T, grad_mlp, preferred_element_type=jnp.float32)
    grad_act = jnp.dot(grad_mlp, down_weight.T, preferred_element_type=jnp.float32)
    unused_value, gelu_back = jax.vjp(gelu_tanh, pre_act)
    grad_pre = gelu_back(grad_act)[0].astype(jnp.bfloat16)
    grad_up = jnp.dot(normal_mid.T, grad_pre, preferred_element_type=jnp.float32)
    mid_part = jnp.dot(grad_pre, up_weight.T, preferred_element_type=jnp.float32)
    grad_mid = lax.psum(mid_part, "tensor").reshape(seq_count, length, width)
    grad_hat_two, scale_grad_two = norm_back(grad_mid, normed_two, inv_two, scale_two)
    grad_hidden = grad_final + grad_hat_two
    grad_second = jnp.dot(one_hot.T, scale_grad_two, precision=highest)
    grad_attn = grad_hidden.astype(jnp.bfloat16).reshape(flat_rows, width)
    grad_merge = jnp.dot(heads_out.T, grad_attn, preferred_element_type=jnp.float32)
    grad_heads = (
        jnp.dot(grad_attn, merge_weight.T, preferred_element_type=jnp.float32)
        .astype(jnp.bfloat16)
        .reshape(head_shape)
    )
    grad_keys = jnp.zeros(head_shape, jnp.float32)
    grad_values = jnp.zeros(head_shape, jnp.float32)
    query_grads = []
    for block_index in range(len(log_sums)):
        offset = block_index * block_rows
        query_block = query_rot[:, offset : offset + block_rows]
        grad_block = grad_heads[:, offset : offset + block_rows]
        scores = block_scores(query_block, key_rot, key_bias, scale_factor)
        soft_weights = jnp.exp(scores - log_sums[block_index])
        grad_soft = jnp.einsum(
            "sqhd,skhd->shqk", grad_block, value_rows, preferred_element_type=jnp.float32
        )
        grad_values = grad_values + jnp.einsum(
            "shqk,sqhd->skhd",
            soft_weights.astype(jnp.bfloat16),
            grad_block,
            preferred_element_type=jnp.float32,
        )
        grad_scores = (
            soft_weights * (grad_soft - jnp.sum(soft_weights * grad_soft, axis=-1, keepdims=True))
        ).astype(jnp.bfloat16)
        query_grads.append(
            jnp.einsum("shqk,skhd->sqhd", grad_scores, key_rot, preferred_element_type=jnp.float32)
            * scale_factor
        )
        grad_keys = (
            grad_keys
            + jnp.einsum(
                "shqk,sqhd->skhd", grad_scores, query_block, preferred_element_type=jnp.float32
            )
            * scale_factor
        )
    query_back = (
        unrotate(jnp.concatenate(query_grads, axis=1), cos_table, sin_table)
        .astype(jnp.bfloat16)
        .reshape(flat_rows, local_width)
    )
    key_back = (
        unrotate(grad_keys, cos_table, sin_table)
        .astype(jnp.bfloat16)
        .reshape(flat_rows, local_width)
    )
    value_back = grad_values.astype(jnp.bfloat16).reshape(flat_rows, local_width)
    grad_query = jnp.dot(normal_in.T, query_back, preferred_element_type=jnp.float32)
    grad_key = jnp.dot(normal_in.T, key_back, preferred_element_type=jnp.float32)
    grad_value = jnp.dot(normal_in.T, value_back, preferred_element_type=jnp.float32)
    inner_part = jnp.dot(query_back, query_weight.T, preferred_element_type=jnp.float32)
    inner_part = inner_part + jnp.dot(key_back, key_weight.T, preferred_element_type=jnp.float32)
    inner_part = inner_part + jnp.dot(
        value_back, value_weight.T, preferred_element_type=jnp.float32
    )
    grad_inner = lax.psum(inner_part, "tensor").reshape(seq_count, length, width)
    grad_hat_one, scale_grad_one = norm_back(grad_inner, normed_one, inv_one, scale_one)
    grad_tokens = ((grad_hidden + grad_hat_one) * row_mask[:, :, None]).astype(jnp.bfloat16)
    grad_first = jnp.dot(one_hot.T, scale_grad_one, precision=highest)
    summed = (
        lax.psum_scatter(grad_query, "dp", scatter_dimension=0, tiled=True),
        lax.psum_scatter(grad_key, "dp", scatter_dimension=0, tiled=True),
        lax.psum_scatter(grad_value, "dp", scatter_dimension=0, tiled=True),
        lax.psum_scatter(grad_merge, "dp", scatter_dimension=1, tiled=True),
        lax.psum_scatter(grad_up, "dp", scatter_dimension=0, tiled=True),
        lax.psum_scatter(grad_down, "dp", scatter_dimension=1, tiled=True),
        lax.psum_scatter(grad_first, "dp", scatter_dimension=1, tiled=True),
        lax.psum_scatter(grad_second, "dp", scatter_dimension=1, tiled=True),
    )
    return (
        layer_output,
        grad_tokens,
        summed[0],
        summed[1],
        summed[2],
        summed[3],
        summed[4],
        summed[5],
        summed[6],
        summed[7],
    )


def solution(mesh):
    return jax.shard_map(
        body,
        mesh=mesh,
        in_specs=(
            P("dp", None, None),
            P("dp", None, None),
            P("dp"),
            P("dp"),
            P(None, "tensor"),
            P(None, "tensor"),
            P(None, "tensor"),
            P("tensor", None),
            P(None, "tensor"),
            P("tensor", None),
            P(),
            P(),
        ),
        out_specs=(
            P("dp", None, None),
            P("dp", None, None),
            P("dp", "tensor"),
            P("dp", "tensor"),
            P("dp", "tensor"),
            P("tensor", "dp"),
            P("dp", "tensor"),
            P("tensor", "dp"),
            P(None, "dp"),
            P(None, "dp"),
        ),
        check_vma=False,
    )
```

profile of v0, /device:TPU:0, one launch (start us, length us, event | category | flops | bytes accessed | tf_op | source)
XLA Modules:
  0.0 1146.7 jit_solution(13432809446621315763)
XLA Ops:
  8.7 2.1 fusion.31
  10.9 2.6 multiply_reduce_fusion.3
  14.0 2.4 copy.24
  16.4 2.3 copy.25
  18.7 1.8 fusion.106
  20.4 1.0 multiply_convert_fusion.5
  21.5 1.3 fusion.54
  23.5 1.3 fusion.51
  25.5 2.6 fusion.104
  28.2 7.5 fusion.105
  35.7 1.3 fusion.59
  37.0 3.5 fusion.1
  40.5 3.8 fusion.67
  44.4 7.8 fusion
  52.2 7.7 fusion.68
  60.7 3.3 convolution_bitcast_fusion.1
  64.1 1.7 fusion.107
  65.7 29.5 %all-reduce.5.cloned.1.call-done = f32[1,1024,1024]{2,1,0:T(8,128)} async-done(((f32[1,1024,1024]{2,1,0:T(8,128)}), f32[1,1024,1024]{2,1,0:T(8,128)}) %all-reduce.5.cloned.1.call-update) | async-done | bytes 4194320 | tf_op jit(solution)/shard_map/psum | solution.py:148
  95.3 2.9 fusion.102
  98.8 1.5 copy-done.3
  100.3 1.6 copy-done.51
  101.9 4.7 fusion.100
  106.6 12.9 %fusion.7 = bf16[1024,2048]{1,0:T(8,128)(2,1)} fusion(f32[1024,2048]{1,0:T(8,128)S(1)} %fusion.100, bf16[2048,1024]{1,0:T(8,128)(2,1)S(1)} %copy-done.52, bf16[1,1024,1024]{2,1,0:T(8,128)(2,1)S(1)} %copy-done.29, f32[1024]{0:T(1024)S(1)} %fusion.89), kind=kOutput, calls=%fused_computation.23 | convolution fusion | flops 4348444672 | bytes 18878464 | tf_op jit(solution)/shard_map/dot_general | solution.py:162
  119.5 8.4 fusion.108
  128.0 11.7 %convolution_bitcast_fusion = f32[1,1024,1024]{2,1,0:T(8,128)} fusion(bf16[2048,1024]{1,0:T(8,128)(2,1)} %param.21, f32[1024,2048]{1,0:T(8,128)} %copy-done.53), kind=kOutput, calls=%fused_computation.65 | convolution fusion | flops 4313841664 | bytes 16777216 | tf_op jit(solution)/shard_map/dot_general | solution.py:154
  139.6 18.0 %all-reduce.7.cloned.1.call-done = f32[1024,1024]{1,0:T(8,128)} async-done(((f32[1024,1024]{1,0:T(8,128)}), f32[1024,1024]{1,0:T(8,128)}) %all-reduce.7.cloned.1.call-update) | async-done | bytes 4194320 | tf_op jit(solution)/shard_map/psum | solution.py:167
  157.7 2.7 multiply_reduce_fusion.5
  161.1 3.8 fusion.18
  165.0 1.8 fusion.27
  166.8 1.3 fusion.62
  168.9 1.0 slice-done.2
  169.9 1.7 slice-done.3
  171.6 4.0 fusion.10
  175.5 7.9 multiply_reduce_fusion
  183.4 11.0 multiply_reduce_fusion.1
  194.4 15.5 %multiply_convert_fusion.1 = bf16[8,512,1024]{2,1,0:T(8,128)(2,1)} fusion(f32[8,512,1024]{2,1,0:T(8,128)} %get-tuple-element.41, f32[8,512,1024]{2,1,0:T(8,128)} %get-tuple-element.39, f32[8,512]{1,0:T(8,128)S(1)} %get-tuple-element.40, f32[8,512]{1,0:T(8,128)S(1)} %log_add_fusion.1), kind=kLoop, calls=%fused_computation.3 | loop fusion | flops 16777216 | bytes 41975808 | tf_op jit(solution)/shard_map/convert_element_type | solution.py:198
  210.0 7.1 fusion.66
  217.1 6.4 fusion.95
  223.5 8.7 add_convert_fusion
  232.2 10.2 multiply_convert_fusion
  242.4 6.2 fusion.65
  248.8 1.6 multiply_bitcast_fusion
  251.6 1.3 fusion.109
  253.3 1.3 fusion.110
  254.8 3.3 add_add_fusion
  258.1 5.3 fusion.35
  263.7 2.7 fusion.45
  266.5 3.9 fusion.43
  270.5 4.9 fusion.47
  275.6 22.8 %all-reduce.9.cloned.1.call-done = (f32[1,1024,1024]{2,1,0:T(8,128)}, f32[1024,1024]{1,0:T(8,128)}) async-done(((f32[1,1024,1024]{2,1,0:T(8,128)}, f32[1024,1024]{1,0:T(8,128)}), (f32[1,1024,1024]{2,1,0:T(8,128)}, f32[1024,1024]{1,0:T(8,128)})) %all-reduce.9.cloned.1.call-update) | async-done | bytes 8388624 | tf_op jit(solution)/shard_map/psum | solution.py:155
  298.3 3.3 fusion.19
  301.7 1.7 broadcast_multiply_fusion
  304.2 11.6 %fusion.98 = f32[1024,2048]{1,0:T(8,128)} fusion(bf16[1024,2048]{1,0:T(8,128)(2,1)} %fusion.7, f32[1,1024,1024]{2,1,0:T(8,128)} %copy-done.3, f32[1024]{0:T(1024)S(1)} %bitcast.212, f32[1024]{0:T(1024)S(1)} %add_rsqrt_fusion, f32[1024]{0:T(1024)S(1)} %broadcast_multiply_fusion.6), kind=kOutput, calls=%fused_computation.155 | convolution fusion | flops 4299161600 | bytes 16789504 | tf_op jit(solution)/shard_map/dot_general | solution.py:165
  316.1 12.0 %fusion.72 = f32[2048,1024]{0,1:T(8,128)} fusion(bf16[1,1024,1024]{2,1,0:T(8,128)(2,1)} %param.13, f32[1024]{0:T(1024)S(1)} %fusion.89, f32[1024,2048]{1,0:T(8,128)} %copy-done.53), kind=kOutput, calls=%fused_computation.117 | convolution fusion | flops 4316987392 | bytes 18878464 | tf_op jit(solution)/shard_map/dot_general | solution.py:161
  328.1 2.7 multiply_reduce_fusion.4
  331.6 7.3 fusion.24
  338.9 43.8 %reduce-scatter.15.cloned.1.call-done = f32[512,64]{0,1:T(8,128)} async-done(((f32[512,1024]{0,1:T(8,128)}), f32[512,64]{0,1:T(8,128)}) %reduce-scatter.15.cloned.1.call-update) | async-done | bytes 131088 | tf_op jit(solution)/shard_map/reduce_scatter | solution.py:237
  382.7 80.6 %reduce-scatter.13.cloned.1.call-done = f32[64,512]{1,0:T(8,128)} async-done(((f32[1024,512]{1,0:T(8,128)}), f32[64,512]{1,0:T(8,128)}) %reduce-scatter.13.cloned.1.call-update) | async-done | bytes 131088 | tf_op jit(solution)/shard_map/reduce_scatter | solution.py:236
  463.3 80.6 %reduce-scatter.9.cloned.1.call-done = f32[64,512]{1,0:T(8,128)} async-done(((f32[1024,512]{1,0:T(8,128)}), f32[64,512]{1,0:T(8,128)}) %reduce-scatter.9.cloned.1.call-update) | async-done | bytes 131088 | tf_op jit(solution)/shard_map/reduce_scatter | solution.py:234
  543.9 80.7 %reduce-scatter.11.cloned.1.call-done = f32[64,512]{1,0:T(8,128)} async-done(((f32[1024,512]{1,0:T(8,128)}), f32[64,512]{1,0:T(8,128)}) %reduce-scatter.11.cloned.1.call-update) | async-done | bytes 131088 | tf_op jit(solution)/shard_map/reduce_scatter | solution.py:235
  624.6 77.9 %reduce-scatter.23.cloned.1.call-done = f32[256,64]{0,1:T(8,128)} async-done(((f32[256,1024]{0,1:T(8,128)}), f32[256,64]{0,1:T(8,128)}) %reduce-scatter.23.cloned.1.call-update) | async-done | bytes 65552 | tf_op jit(solution)/shard_map/reduce_scatter | solution.py:241
  702.5 77.2 %reduce-scatter.21.cloned.1.call-done = f32[256,64]{0,1:T(8,128)} async-done(((f32[256,1024]{0,1:T(8,128)}), f32[256,64]{0,1:T(8,128)}) %reduce-scatter.21.cloned.1.call-update) | async-done | bytes 65552 | tf_op jit(solution)/shard_map/reduce_scatter | solution.py:240
  779.6 177.0 %reduce-scatter.17.cloned.1.call-done = f32[64,2048]{1,0:T(8,128)} async-done(((f32[1024,2048]{1,0:T(8,128)}), f32[64,2048]{1,0:T(8,128)}) %reduce-scatter.17.cloned.1.call-update) | async-done | bytes 524304 | tf_op jit(solution)/shard_map/reduce_scatter | solution.py:238
  956.6 183.1 %reduce-scatter.19.cloned.1.call-done = f32[2048,64]{0,1:T(8,128)} async-done(((f32[2048,1024]{0,1:T(8,128)}), f32[2048,64]{0,1:T(8,128)}) %reduce-scatter.19.cloned.1.call-update) | async-done | bytes 524304 | tf_op jit(solution)/shard_map/reduce_scatter | solution.py:239
  (156 shorter events, 9.5 us)
Async XLA Ops:
  7.2 53.5 %copy-start = (bf16[512,1024]{1,0:T(8,128)(2,1)S(1)}, bf16[512,1024]{1,0:T(8,128)(2,1)}, u32[]{:S(2)}) copy-start(bf16[512,1024]{1,0:T(8,128)(2,1)} %param.19) | copy-start | bytes 3145732
  7.2 88.1 %all-reduce.5.cloned.1.call-start = ((), (), s32[]{:S(2)}) async-start(), calls=%async_computation.8 | async-start | bytes 8388608 | tf_op jit(solution)/shard_map/psum | solution.py:148
  10.8 9.6 copy-start.7
  10.8 10.6 copy-start.45
  13.4 8.0 copy-start.49
  14.0 10.8 copy-start.30
  14.0 10.8 copy-start.32
  18.6 2.8 copy-start.39
  20.4 2.4 copy-start.47
  21.5 14.2 %copy-start.27 = (bf16[1,1024,1024]{2,1,0:T(8,128)(2,1)}, bf16[1,1024,1024]{2,1,0:T(8,128)(2,1)S(1)}, u32[]{:S(2)}) copy-start(bf16[1,1024,1024]{2,1,0:T(8,128)(2,1)S(1)} %multiply_convert_fusion.5) | copy-start | bytes 6291460
  21.5 2.0 copy-start.38
  25.5 2.6 copy-start.12
  25.5 2.6 copy-start.14
  25.5 2.6 copy-start.16
  25.5 2.6 copy-start.18
  28.1 12.4 %copy-start.2 = (f32[8,512,1024]{2,1,0:T(8,128)}, f32[8,512,1024]{2,1,0:T(8,128)S(1)}, u32[]{:S(2)}) copy-start(f32[8,512,1024]{2,1,0:T(8,128)S(1)} %get-tuple-element.37) | copy-start | bytes 50331652
  28.1 7.5 copy-start.34
  37.0 15.2 %copy-start.24 = (bf16[1024,512]{0,1:T(8,128)(2,1)}, bf16[1024,512]{0,1:T(8,128)(2,1)S(1)}, u32[]{:S(2)}) copy-start(bf16[1024,512]{0,1:T(8,128)(2,1)S(1)} %fusion.59) | copy-start | bytes 3145732
  44.4 15.6 %copy-start.43 = (bf16[8,64,512]{2,1,0:T(8,128)(2,1)}, bf16[8,64,512]{2,1,0:T(8,128)(2,1)S(1)}, u32[]{:S(2)}) copy-start(bf16[8,64,512]{2,1,0:T(8,128)(2,1)S(1)} %fusion.67) | copy-start | bytes 1572868
  64.0 93.6 %all-reduce.7.cloned.1.call-start = ((), (), s32[]{:S(2)}) async-start(), calls=%async_computation.9 | async-start | bytes 8388608 | tf_op jit(solution)/shard_map/psum | solution.py:167
  98.2 2.1 copy-start.3
  98.2 3.7 copy-start.51
  101.9 4.7 copy-start.29
  101.9 4.7 copy-start.52
  106.6 12.9 %copy-start.53 = (f32[1024,2048]{1,0:T(8,128)}, f32[1024,2048]{1,0:T(8,128)S(1)}, u32[]{:S(2)}) copy-start(f32[1024,2048]{1,0:T(8,128)S(1)} %fusion.100) | copy-start | bytes 25165828
  127.9 170.4 %all-reduce.9.cloned.1.call-start = ((), (), s32[]{:S(2)}) async-start(), calls=%async_computation.18 | async-start | bytes 16777216 | tf_op jit(solution)/shard_map/psum | solution.py:155
  157.7 3.4 copy-start.4
  161.1 3.9 copy-start.10
  161.1 7.8 slice-start
  165.0 4.0 slice-start.1
  165.0 4.9 slice-start.2
  166.8 2.1 copy-start.9
  166.8 4.8 slice-start.3
  168.9 14.5 %copy-start.21 = (bf16[1024,512]{0,1:T(8,128)(2,1)}, bf16[1024,512]{0,1:T(8,128)(2,1)S(1)}, u32[]{:S(2)}) copy-start(bf16[1024,512]{0,1:T(8,128)(2,1)S(1)} %fusion.62) | copy-start | bytes 3145732
  171.6 4.0 copy-start.25
  194.4 15.5 %copy-start.17 = (bf16[1024,8,32]{0,2,1:T(8,128)(2,1)S(1)}, bf16[1024,8,32]{0,2,1:T(8,128)(2,1)}, u32[]{:S(2)}) copy-start(bf16[1024,8,32]{0,2,1:T(8,128)(2,1)} %copy-done.16) | copy-start | bytes 1572868
  194.4 15.5 %copy-start.19 = (bf16[1024,8,32]{0,2,1:T(8,128)(2,1)S(1)}, bf16[1024,8,32]{0,2,1:T(8,128)(2,1)}, u32[]{:S(2)}) copy-start(bf16[1024,8,32]{0,2,1:T(8,128)(2,1)} %copy-done.18) | copy-start | bytes 1572868
  209.9 7.1 copy-start.13
  209.9 7.1 copy-start.15
  217.1 6.4 copy-start.20
  217.1 6.4 copy-start.22
  242.4 6.2 copy-start.6
  242.4 6.4 copy-start.11
  248.8 1.6 copy-start.31
  248.8 1.6 copy-start.33
  251.3 1.6 copy-start.42
  251.3 1.6 copy-start.40
  251.6 1.7 copy-start.37
  258.1 5.6 copy-start.28
  258.1 124.6 %reduce-scatter.15.cloned.1.call-start = ((), (), s32[]{:S(2)}) async-start(), calls=%async_computation.13 | async-start | bytes 2228224 | tf_op jit(solution)/shard_map/reduce_scatter | solution.py:237
  263.5 199.8 %reduce-scatter.13.cloned.1.call-start = ((), (), s32[]{:S(2)}) async-start(), calls=%async_computation.12 | async-start | bytes 2228224 | tf_op jit(solution)/shard_map/reduce_scatter | solution.py:236
  266.4 4.1 copy-start.41
  266.4 277.5 %reduce-scatter.9.cloned.1.call-start = ((), (), s32[]{:S(2)}) async-start(), calls=%async_computation.10 | async-start | bytes 2228224 | tf_op jit(solution)/shard_map/reduce_scatter | solution.py:234
  270.4 27.9 %copy-start.8 = (bf16[1,1024,1024]{2,1,0:T(8,128)(2,1)S(1)}, bf16[1,1024,1024]{2,1,0:T(8,128)(2,1)}, u32[]{:S(2)}) copy-start(bf16[1,1024,1024]{2,1,0:T(8,128)(2,1)} %param.12) | copy-start | bytes 6291460
  270.4 27.9 %copy-start.46 = (f32[1024]{0:T(1024)S(1)}, f32[1024]{0:T(1024)}, u32[]{:S(2)}) copy-start(f32[1024]{0:T(1024)} %copy-done.45) | copy-start | bytes 12292
  270.4 27.9 %copy-start.48 = (f32[1,1024]{1,0:T(1,128)S(1)}, f32[1,1024]{1,0:T(1,128)}, u32[]{:S(2)}) copy-start(f32[1,1024]{1,0:T(1,128)} %copy-done.47) | copy-start | bytes 12292
  270.4 27.9 %copy-start.50 = (f32[1024]{0:T(1024)S(1)}, f32[1024]{0:T(1024)}, u32[]{:S(2)}) copy-start(f32[1024]{0:T(1024)} %copy-done.49) | copy-start | bytes 12292
  270.5 354.1 %reduce-scatter.11.cloned.1.call-start = ((), (), s32[]{:S(2)}) async-start(), calls=%async_computation.11 | async-start | bytes 2228224 | tf_op jit(solution)/shard_map/reduce_scatter | solution.py:235
  275.5 427.0 %reduce-scatter.23.cloned.1.call-start = ((), (), s32[]{:S(2)}) async-start(), calls=%async_computation.17 | async-start | bytes 1114112 | tf_op jit(solution)/shard_map/reduce_scatter | solution.py:241
  303.4 476.2 %reduce-scatter.21.cloned.1.call-start = ((), (), s32[]{:S(2)}) async-start(), calls=%async_computation.16 | async-start | bytes 1114112 | tf_op jit(solution)/shard_map/reduce_scatter | solution.py:240
  304.2 652.5 %reduce-scatter.17.cloned.1.call-start = ((), (), s32[]{:S(2)}) async-start(), calls=%async_computation.14 | async-start | bytes 8912896 | tf_op jit(solution)/shard_map/reduce_scatter | solution.py:238
  315.8 824.0 %reduce-scatter.19.cloned.1.call-start = ((), (), s32[]{:S(2)}) async-start(), calls=%async_computation.15 | async-start | bytes 8912896 | tf_op jit(solution)/shard_map/reduce_scatter | solution.py:239
  328.1 3.5 copy-start.5
  331.6 808.2 %copy-start.1 = (bf16[512,1024]{1,0:T(8,128)(2,1)S(1)}, bf16[512,1024]{1,0:T(8,128)(2,1)}, u32[]{:S(2)}) copy-start(bf16[512,1024]{1,0:T(8,128)(2,1)} %param.19) | copy-start | bytes 3145732
  (5 other events, 6.5 us)
Sparse Core Ops, SparseCore 0:
  64.1 31.0 all-reduce.4
  128.0 29.5 all-reduce.6
  258.2 40.0 all-reduce.8
  301.0 81.5 reduce-scatter.14
  385.4 77.8 reduce-scatter.12
  466.0 77.8 reduce-scatter.8
  546.7 77.8 reduce-scatter.10
  627.4 74.9 reduce-scatter.22
  705.4 74.1 reduce-scatter.20
  782.3 174.2 reduce-scatter.16
  959.5 180.2 reduce-scatter.18
where the time goes:
time: 1160 us; the launch traced here: 1150 us
  waiting for transfers between devices  872 us (75%)
  matrix products  170 us (15%)
  other arithmetic  71.8 us (6%)
  between operations  16.5 us (1%)
  local copies, waits for them, and re-layouts  15.3 us (1%)
    reduce_scatter x1, waiting for transfers between devices, body(): lax.psum_scatter(grad_down, 'dp', scatter_dimension=1, tiled=True)  183 us
    reduce_scatter x1, waiting for transfers between devices, body(): lax.psum_scatter(grad_up, 'dp', scatter_dimension=0, tiled=True)  177 us
    reduce_scatter x1, waiting for transfers between devices, body(): lax.psum_scatter(grad_key, 'dp', scatter_dimension=0, tiled=True)  80.7 us
    reduce_scatter x1, waiting for transfers between devices, body(): lax.psum_scatter(grad_value, 'dp', scatter_dimension=0, tiled=True)  80.6 us
    reduce_scatter x1, waiting for transfers between devices, body(): lax.psum_scatter(grad_query, 'dp', scatter_dimension=0, tiled=True)  80.6 us
    reduce_scatter x1, waiting for transfers between devices, body(): lax.psum_scatter(grad_second, 'dp', scatter_dimension=1, tiled=True)  77.9 us
    reduce_scatter x1, waiting for transfers between devices, body(): lax.psum_scatter(grad_first, 'dp', scatter_dimension=1, tiled=True)  77.2 us
    reduce_scatter x1, waiting for transfers between devices, body(): lax.psum_scatter(grad_merge, 'dp', scatter_dimension=1, tiled=True)  43.8 us
  transfers between devices with their start and end apart: 11, of which 11 were waited for; matrix products, arithmetic and copies ran while one was open for 6% of the time, Pallas kernels for 0%

commit v1 on v0

--- a/solution.py
+++ b/solution.py
@@ -1,11 +1,166 @@
+import functools
 import math
 
 import jax
 import jax.numpy as jnp
 from jax import lax
+from jax.experimental import pallas as pl
+from jax.experimental.pallas import tpu as pltpu
 from jax.sharding import PartitionSpec as P
 
 HEAD = 64
+MESH = pl.DeviceIdType.MESH
+
+NI = 24
+TILE = 256
+SR = 6
+LAGS = (4, 7, 9, 11)
+
+def group_of(i):
+    one = lambda k: jnp.where(i >= k, 1, 0)
+    return one(8) + one(16) + one(18)
+
+def flip(d, w):
+    return d + w * (1 - 2 * (lax.rem(lax.div(d, w), 2)))
+
+def weight(c, s):
+    k = lax.rem(c + s, 3)
+    return 1 + (k * (k + 1)) // 2
+
+def color_of(i):
+    return lax.rem(lax.rem(i, 8), 3)
+
+def grads_kernel(names, l0, l1, l2, l3, r0, r1, r2, r3, out,
+           L, S1, R1, R2, R3, R4, rb, lsem, rsem, ssem, csem):
+    d = lax.axis_index(names[0])
+    t = lax.axis_index(names[1])
+    lrefs = (l0, l1, l2, l3)
+    rrefs = (r0, r1, r2, r3)
+    def absolute(r):
+        o = 0
+        for b in range(4):
+            db = lax.rem(lax.div(d, 2 ** b), 2)
+            o = o + (2 ** b) * (db if not (r >> b) & 1 else 1 - db)
+        return o
+    loads = []
+    for g in range(4):
+        for r in range(16):
+            c = pltpu.make_async_copy(lrefs[g].at[absolute(r)], L.at[g, r], lsem.at[g])
+            c.start()
+    bar = pltpu.get_barrier_semaphore()
+    for w in (1, 2, 4, 8):
+        pl.semaphore_signal(bar, inc=1, device_id=(flip(d, w), t), device_id_type=MESH)
+    pl.semaphore_wait(bar, 4)
+
+    def fetch(i, lane):
+        firsts = (0, 8, 16, 18, 24)
+        for g in range(4):
+            @pl.when((i >= firsts[g]) & (i < firsts[g + 1]))
+            def _():
+                col = pl.multiple_of((i - firsts[g]) * TILE, TILE)
+                pltpu.make_async_copy(rrefs[g].at[:, pl.ds(col, TILE)], rb.at[lane, lax.rem(i, 2)], rsem.at[lane, lax.rem(i, 2)]).start()
+    def fetched(i, lane):
+        pltpu.make_async_copy(r0.at[:, pl.ds(0, TILE)], rb.at[lane, lax.rem(i, 2)], rsem.at[lane, lax.rem(i, 2)]).wait()
+
+    def product(i, first, lane):
+        c = color_of(i)
+        g = group_of(i)
+        ws = [weight(c, s) for s in range(3)] + [8]
+        rows = []
+        for b2 in (0, 1):
+            for b3 in (0, 1):
+                for b4 in (0, 1):
+                    r = first * ws[0] + b2 * ws[1] + b3 * ws[2] + b4 * ws[3]
+                    rows.append(L[g, r])
+        lhs = jnp.concatenate(rows, axis=0)
+        return jnp.dot(lhs, rb[lane, lax.rem(i, 2)], preferred_element_type=jnp.float32).reshape(8, 64, TILE)
+
+    def copy(i, s):
+        c = color_of(i)
+        w = weight(c, s) if s < 3 else 8
+        src = (S1.at[lax.rem(i, SR)], R1.at[i, pl.ds(4, 4)], R2.at[i, pl.ds(2, 2)], R3.at[i, pl.ds(1, 1)])[s]
+        dst = (R1.at[i], R2.at[i], R3.at[i], R4.at[i])[s]
+        return pltpu.make_async_remote_copy(src_ref=src, dst_ref=dst, send_sem=ssem.at[s, i], recv_sem=csem.at[s, i],
+                                            device_id=(flip(d, w), t), device_id_type=MESH)
+
+    fetch(0, 0)
+    fetch(0, 1)
+    for g in range(4):
+        pltpu.make_async_copy(L.at[g], L.at[g], lsem.at[g]).wait()
+
+    def body(i, _):
+        @pl.when(i < NI)
+        def _():
+            @pl.when(i + 1 < NI)
+            def _():
+                fetch(i + 1, 0)
+            @pl.when(i >= SR)
+            def _():
+                copy(i - SR, 0).wait_send()
+            fetched(i, 0)
+            S1[lax.rem(i, SR)] = product(i, 1, 0)
+            copy(i, 0).start()
+        j = i - LAGS[0]
+        @pl.when((j >= 0) & (j < NI))
+        def _():
+            @pl.when(j + 1 < NI)
+            def _():
+                fetch(j + 1, 1)
+            fetched(j, 1)
+            copy(j, 0).wait_recv()
+            R1[j] += product(j, 0, 1)
+            copy(j, 1).start()
+        k = i - LAGS[1]
+        @pl.when((k >= 0) & (k < NI))
+        def _():
+            copy(k, 1).wait_recv()
+            R2[k] += R1[k, 0:4]
+            copy(k, 2).start()
+        m = i - LAGS[2]
+        @pl.when((m >= 0) & (m < NI))
+        def _():
+            copy(m, 2).wait_recv()
+            R3[m] += R2[m, 0:2]
+            copy(m, 3).start()
+        n = i - LAGS[3]
+        @pl.when((n >= 0) & (n < NI))
+        def _():
+            copy(n, 3).wait_recv()
+            out[n] = R4[n, 0] + R3[n, 0]
+        return 0
+    lax.fori_loop(0, NI + LAGS[3], body, 0)
+    def drain(i, _):
+        @pl.when(i >= NI - SR)
+        def _():
+            copy(i, 0).wait_send()
+        for s in (1, 2, 3):
+            copy(i, s).wait_send()
+        return 0
+    lax.fori_loop(0, NI, drain, 0)
+
+def reduce_grads(names, lhs, rhs):
+    ANY = pl.BlockSpec(memory_space=pl.ANY)
+    return pl.pallas_call(
+        functools.partial(grads_kernel, names),
+        out_shape=jax.ShapeDtypeStruct((NI, 64, TILE), jnp.float32),
+        in_specs=[ANY] * 8,
+        out_specs=pl.BlockSpec(memory_space=pltpu.VMEM),
+        scratch_shapes=[
+            pltpu.VMEM((4, 16, 64, 1024), jnp.bfloat16),
+            pltpu.VMEM((SR, 8, 64, TILE), jnp.float32),
+            pltpu.VMEM((NI, 8, 64, TILE), jnp.float32),
+            pltpu.VMEM((NI, 4, 64, TILE), jnp.float32),
+            pltpu.VMEM((NI, 2, 64, TILE), jnp.float32),
+            pltpu.VMEM((NI, 1, 64, TILE), jnp.float32),
+            pltpu.VMEM((2, 2, 1024, TILE), jnp.bfloat16),
+            pltpu.SemaphoreType.DMA((4,)),
+            pltpu.SemaphoreType.DMA((2, 2)),
+            pltpu.SemaphoreType.DMA((4, NI)),
+            pltpu.SemaphoreType.DMA((4, NI)),
+        ],
+        compiler_params=pltpu.CompilerParams(collective_id=0, has_side_effects=True, vmem_limit_bytes=56 * 2**20),
+        name="grads",
+    )(*lhs, *rhs)
 
 
 epsilon = 1e-05
@@ -158,18 +313,14 @@
     ).astype(jnp.bfloat16)
     grad_final = cotangent.astype(jnp.float32) * row_mask[:, :, None]
     grad_mlp = grad_final.astype(jnp.bfloat16).reshape(flat_rows, width)
-    grad_down = jnp.dot(activated.T, grad_mlp, preferred_element_type=jnp.float32)
     grad_act = jnp.dot(grad_mlp, down_weight.T, preferred_element_type=jnp.float32)
     unused_value, gelu_back = jax.vjp(gelu_tanh, pre_act)
     grad_pre = gelu_back(grad_act)[0].astype(jnp.bfloat16)
-    grad_up = jnp.dot(normal_mid.T, grad_pre, preferred_element_type=jnp.float32)
     mid_part = jnp.dot(grad_pre, up_weight.T, preferred_element_type=jnp.float32)
     grad_mid = lax.psum(mid_part, "tensor").reshape(seq_count, length, width)
     grad_hat_two, scale_grad_two = norm_back(grad_mid, normed_two, inv_two, scale_two)
     grad_hidden = grad_final + grad_hat_two
-    grad_second = jnp.dot(one_hot.T, scale_grad_two, precision=highest)
     grad_attn = grad_hidden.astype(jnp.bfloat16).reshape(flat_rows, width)
-    grad_merge = jnp.dot(heads_out.T, grad_attn, preferred_element_type=jnp.float32)
     grad_heads = (
         jnp.dot(grad_attn, merge_weight.T, preferred_element_type=jnp.float32)
         .astype(jnp.bfloat16)
@@ -218,9 +369,6 @@
         .reshape(flat_rows, local_width)
     )
     value_back = grad_values.astype(jnp.bfloat16).reshape(flat_rows, local_width)
-    grad_query = jnp.dot(normal_in.T, query_back, preferred_element_type=jnp.float32)
-    grad_key = jnp.dot(normal_in.T, key_back, preferred_element_type=jnp.float32)
-    grad_value = jnp.dot(normal_in.T, value_back, preferred_element_type=jnp.float32)
     inner_part = jnp.dot(query_back, query_weight.T, preferred_element_type=jnp.float32)
     inner_part = inner_part + jnp.dot(key_back, key_weight.T, preferred_element_type=jnp.float32)
     inner_part = inner_part + jnp.dot(
@@ -229,28 +377,46 @@
     grad_inner = lax.psum(inner_part, "tensor").reshape(seq_count, length, width)
     grad_hat_one, scale_grad_one = norm_back(grad_inner, normed_one, inv_one, scale_one)
     grad_tokens = ((grad_hidden + grad_hat_one) * row_mask[:, :, None]).astype(jnp.bfloat16)
-    grad_first = jnp.dot(one_hot.T, scale_grad_one, precision=highest)
-    summed = (
-        lax.psum_scatter(grad_query, "dp", scatter_dimension=0, tiled=True),
-        lax.psum_scatter(grad_key, "dp", scatter_dimension=0, tiled=True),
-        lax.psum_scatter(grad_value, "dp", scatter_dimension=0, tiled=True),
-        lax.psum_scatter(grad_merge, "dp", scatter_dimension=1, tiled=True),
-        lax.psum_scatter(grad_up, "dp", scatter_dimension=0, tiled=True),
-        lax.psum_scatter(grad_down, "dp", scatter_dimension=1, tiled=True),
-        lax.psum_scatter(grad_first, "dp", scatter_dimension=1, tiled=True),
-        lax.psum_scatter(grad_second, "dp", scatter_dimension=1, tiled=True),
-    )
+    lhs = (grad_mlp, normal_mid, grad_attn, normal_in)
+    rhs = (activated, grad_pre, heads_out, jnp.concatenate([query_back, key_back, value_back], axis=1))
+    chunks = lax.axis_size("dp")
+    if chunks == 16:
+        pieces = reduce_grads(
+            ("dp", "tensor"), [a.T.reshape(chunks, width // chunks, flat_rows) for a in lhs], rhs
+        )
+        wide = lambda a: a.transpose(1, 0, 2).reshape(width // chunks, -1)
+        sums = [wide(pieces[a:b]) for a, b in ((0, 8), (8, 16), (16, 18), (18, 24))]
+    else:
+        sums = [
+            lax.psum_scatter(
+                jnp.dot(a.T, b, preferred_element_type=jnp.float32), "dp", scatter_dimension=0, tiled=True
+            )
+            for a, b in zip(lhs, rhs)
+        ]
+    grad_down, grad_up, grad_merge, grad_qkv = sums
+    grad_query, grad_key, grad_value = jnp.split(grad_qkv, 3, axis=1)
+    table_terms = jnp.concatenate(
+        [scale_grad_one, scale_grad_two, jnp.zeros((seq_count, 128), jnp.float32) + noise_times.astype(jnp.float32)[:, None]], axis=1
+    )
+    gathered = lax.all_gather(table_terms, "dp", axis=0, tiled=True)
+    mine = lax.axis_index("dp") * (width // chunks)
+    hits = (gathered[:, 2 * width][None, :] == jnp.arange(table_rows, dtype=jnp.float32)[:, None]).astype(jnp.float32)
+    columns = jnp.concatenate(
+        [lax.dynamic_slice_in_dim(gathered, k * width + mine, width // chunks, axis=1) for k in (0, 1)], axis=1
+    )
+    tables = jnp.dot(hits, columns, precision=highest)
+    grad_first, grad_second = jnp.split(tables, 2, axis=1)
     return (
         layer_output,
         grad_tokens,
-        summed[0],
-        summed[1],
-        summed[2],
-        summed[3],
-        summed[4],
-        summed[5],
-        summed[6],
-        summed[7],
+        grad_query,
+        grad_key,
+        grad_value,
+        grad_merge.T,
+        grad_up,
+        grad_down.T,
+        grad_first,
+        grad_second,
     )
 
 

time: 1160 us -> 582 us (0.50)
  waiting for transfers between devices: 872 us -> 49.1 us
  Pallas kernels: 0 us -> 199 us
  local copies, waits for them, and re-layouts: 15.3 us -> 55.7 us
  matrix products: 170 us -> 130 us
  blocking collectives: 0 us -> 39.3 us
    reduce_scatter x8 -> x0, waiting for transfers between devices: 801 us -> none  [the longest x1 183 us: body(): lax.psum_scatter(grad_down, 'dp', scatter_dimension=1, tiled=True)]
    pallas_call x0 -> x1, Pallas kernels: none -> 199 us  [reduce_grads(): pl.pallas_call(functools.partial(grads_kernel, names), out_shape=jax.Shap...]
    dot_general x6 -> x1, matrix products: 40.4 us -> 0.34 us  [body(): tables = jnp.dot(hits, columns, precision=highest)]
    all_gather x0 -> x1, blocking collectives: none -> 39.3 us  [body(): gathered = lax.all_gather(table_terms, 'dp', axis=0, tiled=True)]
    psum x1, waiting for transfers between devices: 22.8 us -> 0.01 us  [body(): mlp_total = lax.psum(mlp_part, 'tensor')]
    transpose x0 -> x4, local copies, waits for them, and re-layouts: none -> 16.1 us  [body(): a.T.reshape(chunks, width // chunks, flat_rows)]
    reduce_sum x2, other arithmetic: 7.15 us -> 18.8 us  [norm_back(): grad_scale = jnp.sum(grad_norm * normed, axis=1)]
    unnamed x118 -> x120, local copies, waits for them, and re-layouts: 15.3 us -> 25.2 us
  transfers between devices with their start and end apart: 11 -> 3, of which waited for: 11 -> 2; matrix products, arithmetic and copies ran while one was open for 6% -> 8% of each run, Pallas kernels for 0% -> 35%
where the time goes in v1:
time: 582 us; the launch traced here: 572 us
  Pallas kernels  199 us (34%)
  matrix products  130 us (22%)
  other arithmetic  82.1 us (14%)
  local copies, waits for them, and re-layouts  55.7 us (10%)
  waiting for transfers between devices  49.1 us (8%)
  blocking collectives  39.3 us (7%)
  between operations  16.3 us (3%)
    pallas_call x1, Pallas kernels, reduce_grads(): pl.pallas_call(functools.partial(grads_kernel, names), out_shape=jax.Shap...  199 us
    all_gather x1, blocking collectives, body(): gathered = lax.all_gather(table_terms, 'dp', axis=0, tiled=True)  39.3 us
    psum x1, waiting for transfers between devices, body(): attn_total = lax.psum(attn_part, 'tensor')  29.6 us
    unnamed x120, local copies, waits for them, and re-layouts  25.2 us
    convert_element_type x2, other arithmetic, body(): grad_scores = (soft_weights * (grad_soft - jnp.sum(soft_weights * grad_so...  22.4 us
    psum x1, waiting for transfers between devices, body(): grad_mid = lax.psum(mid_part, 'tensor').reshape(seq_count, length, width)  19.5 us
    dot_general x2, matrix products, body(): jnp.einsum('sqhd,skhd->shqk', grad_block, value_rows, preferred_element_t...  18.9 us
    reduce_sum x2, other arithmetic, norm_back(): grad_scale = jnp.sum(grad_norm * normed, axis=1)  18.8 us
  transfers between devices with their start and end apart: 3, of which 2 were waited for; matrix products, arithmetic and copies ran while one was open for 8% of the time, Pallas kernels for 35%

profile of v1, /device:TPU:0, one launch (start us, length us, event | category | flops | bytes accessed | tf_op | source)
XLA Modules:
  0.0 571.5 jit_solution(9562023805936834704)
XLA Ops:
  8.0 2.1 fusion.31
  10.2 2.6 multiply_reduce_fusion.3
  13.5 2.3 copy.63
  15.7 2.3 copy.64
  18.0 1.8 fusion.101
  19.8 1.0 multiply_convert_fusion.5
  20.8 1.3 fusion.47
  22.2 1.3 fusion.50
  24.8 2.6 fusion.100
  27.4 7.5 %fusion.99 = (f32[8,512]{1,0:T(8,128)S(1)}, f32[8,512,1024]{2,1,0:T(8,128)}) fusion(f32[1024]{0:T(1024)S(1)} %add_multiply_fusion, bf16[1024,8,32]{0,2,1:T(8,128)(2,1)S(1)} %get-tuple-element.26, bf16[1024,8,32]{0,2,1:T(8,128)(2,1)S(1)} %get-tuple-element.25, bf16[1,1024,8,32]{1,3,2,0:T(8,128)(2,1)S(1)} %get-tuple-element.37, ...), kind=kOutput, calls=%fused_computation.165 | convolution fusion | flops 552595456 | bytes 18894848 | tf_op jit(solution)/shard_map/sqhd,skhd->shqk/dot_general | solution.py:233
  35.0 1.3 fusion.55
  36.3 3.5 fusion
  39.8 4.5 fusion.64
  44.3 2.0 copy.65
  46.4 8.0 %fusion.1 = f32[8,512]{1,0:T(8,128)S(1)} fusion(f32[8,512,1024]{2,1,0:T(8,128)} %get-tuple-element.48, f32[8,512]{1,0:T(8,128)S(1)} %get-tuple-element.47), kind=kLoop, calls=%fused_computation.13 | loop fusion | flops 8384512 | bytes 16809984 | tf_op jit(solution)/shard_map/reduce_sum | solution.py:291
  54.4 8.2 %fusion.63 = bf16[8,64,512]{2,1,0:T(8,128)(2,1)} fusion(bf16[1024,8,64]{0,2,1:T(8,128)(2,1)S(1)} %bitcast.230, f32[8,512,1024]{2,1,0:T(8,128)} %get-tuple-element.48, f32[8,512]{1,0:T(8,128)S(1)} %fusion.1, f32[8,512]{1,0:T(8,128)S(1)} %get-tuple-element.47), kind=kOutput, calls=%fused_computation.92 | convolution fusion | flops 549715968 | bytes 18382848 | tf_op jit(solution)/shard_map/shqk,skhd->sqhd/dot_general | solution.py:295
  62.5 2.0 copy.66
  64.6 4.5 convolution_bitcast_fusion.1
  69.1 1.7 fusion.102
  70.8 29.6 %all-reduce.5.cloned.1.call-done = f32[1,1024,1024]{2,1,0:T(8,128)} async-done(((f32[1,1024,1024]{2,1,0:T(8,128)}), f32[1,1024,1024]{2,1,0:T(8,128)}) %all-reduce.5.cloned.1.call-update) | async-done | bytes 4194320 | tf_op jit(solution)/shard_map/psum | solution.py:303
  100.4 2.9 fusion.95
  103.9 3.1 copy-done.51
  107.0 9.3 %multiply_convert_fusion.2 = (bf16[1024,2048]{1,0:T(8,128)(2,1)}, f32[1024,2048]{1,0:T(8,128)}) fusion(bf16[1024,2048]{1,0:T(8,128)(2,1)S(1)} %copy-done.51, f32[1024]{0:T(1024)S(1)} %bitcast.251, f32[1024]{0:T(1024)S(1)} %add_rsqrt_fusion, f32[1,1024,1024]{2,1,0:T(8,128)S(1)} %get-tuple-element.19, f32[1024]{0:T(1024)S(1)} %broadcast_multiply_fusion.4), kind=kOutput, calls=%fused_computation.30 | convolution fusion | flops 4318035968 | bytes 20983808 | tf_op jit(solution)/shard_map/dot_general | solution.py:307
  116.3 13.1 %fusion.7.r1 = bf16[1024,2048]{1,0:T(8,128)(2,1)S(1)} fusion(f32[1024,2048]{1,0:T(8,128)} %get-tuple-element.52, bf16[2048,1024]{1,0:T(8,128)(2,1)S(1)} %copy-done.52, bf16[1,1024,1024]{2,1,0:T(8,128)(2,1)S(1)} %copy-done.34, f32[1024]{0:T(1024)S(1)} %fusion.86), kind=kOutput, calls=%fused_computation.23 | convolution fusion | flops 4348444672 | bytes 18878464 | tf_op jit(solution)/shard_map/dot_general | solution.py:316
  129.4 2.0 copy-done.33
  131.4 6.1 %fusion.103 = f32[1024,1024]{1,0:T(8,128)} fusion(bf16[1024,2048]{1,0:T(8,128)(2,1)S(1)} %fusion.7.r1, bf16[1024,2048]{1,0:T(8,128)(2,1)S(1)} %copy-done.51), kind=kOutput, calls=%fused_computation.169 | convolution fusion | flops 4294967296 | bytes 12582912 | tf_op jit(solution)/shard_map/dot_general | solution.py:319
  137.6 10.1 %convolution_bitcast_fusion = f32[1,1024,1024]{2,1,0:T(8,128)} fusion(bf16[1024,2048]{1,0:T(8,128)(2,1)} %get-tuple-element.51.r0, bf16[2048,1024]{1,0:T(8,128)(2,1)} %param.21), kind=kOutput, calls=%fused_computation.66 | convolution fusion | flops 4294967296 | bytes 12582912 | tf_op jit(solution)/shard_map/dot_general | solution.py:309
  147.7 19.5 %all-reduce.7.cloned.1.call-done = f32[1024,1024]{1,0:T(8,128)} async-done(((f32[1024,1024]{1,0:T(8,128)}), f32[1024,1024]{1,0:T(8,128)}) %all-reduce.7.cloned.1.call-update) | async-done | bytes 4194320 | tf_op jit(solution)/shard_map/psum | solution.py:320
  167.2 15.3 %fusion.18 = (f32[1024]{0:T(1024)S(1)}, f32[1024]{0:T(1024)S(1)}, bf16[1024,1024]{0,1:T(8,128)(2,1)}) fusion(f32[1024,1024]{1,0:T(8,128)} %all-reduce.7.cloned.1.call-done, f32[1,1024,1024]{2,1,0:T(8,128)} %copy-done.3, f32[1024]{0:T(1024)S(1)} %add_rsqrt_fusion, f32[1024]{0:T(1024)S(1)} %broadcast_multiply_fusion.4, f32[1024]{0:T(1024)S(1)} %bitcast.252), kind=kLoop, calls=%fused_computation.34 | loop fusion | flops 9435136 | bytes 10506240 | tf_op jit(solution)/shard_map/reduce_sum | solution.py:226
  182.9 1.8 copy-done.4
  184.7 3.5 convert_bitcast_fusion
  188.3 1.3 fusion.58
  190.7 2.1 slice-done.2
  192.8 1.2 slice-done.3
  193.9 4.0 fusion.10
  198.0 7.9 %multiply_reduce_fusion = (f32[8,512]{1,0:T(8,128)S(1)}, f32[8,512,1024]{2,1,0:T(8,128)}) fusion(f32[8,512,1024]{2,1,0:T(8,128)S(1)} %bitcast.218, f32[8,512]{1,0:T(8,128)S(1)} %log_add_fusion, bf16[1024,8,64]{0,2,1:T(8,128)(2,1)S(1)} %bitcast.231, bf16[1,1024,8,64]{1,3,2,0:T(8,128)(2,1)S(1)} %bitcast.226), kind=kOutput, calls=%fused_computation.1 | convolution fusion | flops 549449728 | bytes 35160064 | tf_op jit(solution)/shard_map/sqhd,skhd->shqk/dot_general | solution.py:338
  205.9 11.0 %multiply_reduce_fusion.1 = (f32[8,512]{1,0:T(8,128)S(1)}, f32[8,512,1024]{2,1,0:T(8,128)}) fusion(f32[8,512,1024]{2,1,0:T(8,128)} %copy-done.2, f32[8,512]{1,0:T(8,128)S(1)} %log_add_fusion.1, bf16[1024,8,64]{0,2,1:T(8,128)(2,1)S(1)} %bitcast.232, bf16[1,1024,8,64]{1,3,2,0:T(8,128)(2,1)S(1)} %bitcast.227), kind=kOutput, calls=%fused_computation.4 | convolution fusion | flops 549449728 | bytes 35160064 | tf_op jit(solution)/shard_map/sqhd,skhd->shqk/dot_general | solution.py:338
  216.9 12.0 %multiply_convert_fusion.1 = bf16[8,512,1024]{2,1,0:T(8,128)(2,1)S(1)} fusion(f32[8,512,1024]{2,1,0:T(8,128)} %get-tuple-element.54, f32[8,512,1024]{2,1,0:T(8,128)} %copy-done.2, f32[8,512]{1,0:T(8,128)S(1)} %get-tuple-element.53, f32[8,512]{1,0:T(8,128)S(1)} %log_add_fusion.1), kind=kLoop, calls=%fused_computation.3 | loop fusion | flops 16777216 | bytes 41975808 | tf_op jit(solution)/shard_map/convert_element_type | solution.py:349
  228.9 3.2 copy-done.7
  232.2 2.9 fusion.90
  235.2 7.1 %fusion.62 = f32[1,512,8,64]{1,3,2,0:T(8,128)} fusion(bf16[8,512,1024]{2,1,0:T(8,128)(2,1)} %copy-done.7, bf16[1024,8,32]{0,2,1:T(8,128)(2,1)S(1)} %copy-done.21, bf16[1024,8,32]{0,2,1:T(8,128)(2,1)S(1)} %copy-done.19), kind=kOutput, calls=%fused_computation.91 | convolution fusion | flops 539230208 | bytes 10485760 | tf_op jit(solution)/shard_map/shqk,skhd->sqhd/dot_general | solution.py:351
  242.3 8.5 %add_convert_fusion = bf16[8,64,1024]{2,1,0:T(8,128)(2,1)} fusion(f32[8,64,1024]{2,1,0:T(8,128)S(1)} %copy-done.23, f32[8,512,1024]{2,1,0:T(8,128)} %copy-done.2, f32[8,512]{1,0:T(8,128)S(1)} %log_add_fusion.1, bf16[1,1024,8,64]{1,3,2,0:T(8,128)(2,1)S(1)} %bitcast.228), kind=kOutput, calls=%fused_computation.82 | convolution fusion | flops 546308096 | bytes 20463616 | tf_op jit(solution)/shard_map/shqk,sqhd->skhd/dot_general | solution.py:341
  250.8 10.4 %multiply_convert_fusion = bf16[8,512,1024]{2,1,0:T(8,128)(2,1)} fusion(f32[8,512,1024]{2,1,0:T(8,128)} %get-tuple-element.56, f32[8,512,1024]{2,1,0:T(8,128)S(1)} %bitcast.218, f32[8,512]{1,0:T(8,128)S(1)} %get-tuple-element.55, f32[8,512]{1,0:T(8,128)S(1)} %log_add_fusion), kind=kLoop, calls=%fused_computation | loop fusion | flops 16777216 | bytes 41975808 | tf_op jit(solution)/shard_map/convert_element_type | solution.py:349
  261.3 6.2 %fusion.61 = f32[1,512,8,64]{1,3,2,0:T(8,128)S(1)} fusion(bf16[8,512,1024]{2,1,0:T(8,128)(2,1)} %multiply_convert_fusion, bf16[1024,8,32]{0,2,1:T(8,128)(2,1)S(1)} %copy-done.21, bf16[1024,8,32]{0,2,1:T(8,128)(2,1)S(1)} %copy-done.19), kind=kOutput, calls=%fused_computation.89 | convolution fusion | flops 539230208 | bytes 10485760 | tf_op jit(solution)/shard_map/shqk,skhd->sqhd/dot_general | solution.py:351
  267.6 1.6 multiply_bitcast_fusion
  270.5 1.3 fusion.105
  271.9 1.3 fusion.104
  273.8 3.3 add_add_fusion
  277.2 1.6 copy-done.9
  278.7 2.0 fusion.135
  280.7 3.9 copy.70
  284.7 2.3 pad_maximum_fusion.3.r2
  287.0 1.3 copy.73
  288.3 2.4 copy.72
  290.7 2.6 copy.71
  293.3 4.0 copy.67
  297.3 4.1 copy.69
  301.3 4.1 copy.68
  305.4 3.1 pad_maximum_fusion.r3
  308.5 198.9 %grads.1 = f32[24,64,256]{2,1,0:T(8,128)} custom-call(bf16[16,64,1024]{2,1,0:T(8,128)(2,1)} %bitcast.222, bf16[16,64,1024]{2,1,0:T(8,128)(2,1)} %bitcast.224, bf16[16,64,1024]{2,1,0:T(8,128)(2,1)} %bitcast.223, bf16[16,64,1024]{2,1,0:T(8,128)(2,1)} %bitcast.221, bf16[1024,2048]{1,0:T(8,128)(2,1)} %get-tuple-element.51.r0, bf16[1024,2048]{1,0:T(8,128)(2,1)} %copy-done.33, ...), custom_call_target="tpu_custom_call" | custom-call | tf_op jit(solution)/shard_map/grads/pallas_call | solution.py:143
  507.4 1.3 slice_bitcast_fusion.2
  513.7 3.5 fusion.19
  517.6 39.3 %all-gather = f32[16,1,2176]{2,1,0:T(1,128)S(1)} all-gather(f32[1,1,2176]{2,1,0:T(1,128)S(1)} %fusion.82), channel_id=1, replica_groups=mesh['dp'=16,'tensor'=2] {'dp'}, dimensions={0}, use_global_device_ids=true | all-gather | bytes 147968 | tf_op jit(solution)/shard_map/all_gather | solution.py:401
  558.2 6.4 %fusion.24 = (bf16[1,1024,1024]{2,1,0:T(8,128)(2,1)}, bf16[1,1024,1024]{2,1,0:T(8,128)(2,1)}) fusion(f32[1,1024,1024]{2,1,0:T(8,128)} %copy-done.13, bf16[1,1024,1024]{2,1,0:T(8,128)(2,1)S(1)} %copy-done.9, f32[1024,1024]{1,0:T(8,128)S(1)} %copy-done.11, f32[1024]{0:T(1024)S(1)} %broadcast_multiply_fusion, f32[1024]{0:T(1024)S(1)} %broadcast_multiply_fusion.1, ...), kind=kLoop, calls=%fused_computation.43 | loop fusion | flops 15728640 | bytes 23093248 | tf_op jit(solution)/shard_map/convert_element_type | solution.py:379
  (152 shorter events, 12.3 us)
Async XLA Ops:
  7.2 57.4 %copy-start = (bf16[512,1024]{1,0:T(8,128)(2,1)S(1)}, bf16[512,1024]{1,0:T(8,128)(2,1)}, u32[]{:S(2)}) copy-start(bf16[512,1024]{1,0:T(8,128)(2,1)} %param.19) | copy-start | bytes 3145732
  7.2 93.2 %all-reduce.5.cloned.1.call-start = ((), (), s32[]{:S(2)}) async-start(), calls=%async_computation | async-start | bytes 8388608 | tf_op jit(solution)/shard_map/psum | solution.py:303
  10.1 9.6 %copy-start.8 = (bf16[1,1024,1024]{2,1,0:T(8,128)(2,1)S(1)}, bf16[1,1024,1024]{2,1,0:T(8,128)(2,1)}, u32[]{:S(2)}) copy-start(bf16[1,1024,1024]{2,1,0:T(8,128)(2,1)} %param.12) | copy-start | bytes 6291460
  10.2 10.6 %copy-start.45 = (f32[1024]{0:T(1024)}, f32[1024]{0:T(1024)S(1)}, u32[]{:S(2)}) copy-start(f32[1024]{0:T(1024)S(1)} %broadcast_multiply_fusion.5) | copy-start | bytes 12292
  12.8 8.0 %copy-start.49 = (f32[1024]{0:T(1024)}, f32[1024]{0:T(1024)S(1)}, u32[]{:S(2)}) copy-start(f32[1024]{0:T(1024)S(1)} %add_rsqrt_fusion.1) | copy-start | bytes 12292
  18.0 2.8 copy-start.44
  19.8 2.4 copy-start.47
  20.8 1.3 copy-start.43
  24.0 3.3 copy-start.35
  24.0 3.3 copy-start.37
  24.7 2.6 copy-start.14
  24.7 2.6 copy-start.16
  24.8 2.6 copy-start.18
  24.8 2.6 copy-start.20
  27.4 12.4 %copy-start.2 = (f32[8,512,1024]{2,1,0:T(8,128)}, f32[8,512,1024]{2,1,0:T(8,128)S(1)}, u32[]{:S(2)}) copy-start(f32[8,512,1024]{2,1,0:T(8,128)S(1)} %get-tuple-element.50) | copy-start | bytes 50331652
  27.4 7.5 %copy-start.39 = (bf16[1024,512]{1,0:T(8,128)(2,1)S(1)}, bf16[1024,512]{1,0:T(8,128)(2,1)}, u32[]{:S(2)}) copy-start(bf16[1024,512]{1,0:T(8,128)(2,1)} %param.18) | copy-start | bytes 3145732
  36.3 3.6 copy-start.26
  46.4 8.0 %copy-start.27 = (bf16[1024,512]{0,1:T(8,128)(2,1)S(1)}, bf16[1024,512]{0,1:T(8,128)(2,1)}, u32[]{:S(2)}) copy-start(bf16[1024,512]{0,1:T(8,128)(2,1)} %copy-done.26) | copy-start | bytes 3145732
  69.1 98.1 %all-reduce.7.cloned.1.call-start = ((), (), s32[]{:S(2)}) async-start(), calls=%async_computation.1 | async-start | bytes 8388608 | tf_op jit(solution)/shard_map/psum | solution.py:320
  103.3 13.0 %copy-start.3 = (f32[1,1024,1024]{2,1,0:T(8,128)}, f32[1,1024,1024]{2,1,0:T(8,128)S(1)}, u32[]{:S(2)}) copy-start(f32[1,1024,1024]{2,1,0:T(8,128)S(1)} %get-tuple-element.19) | copy-start | bytes 12582916
  103.3 3.7 copy-start.51
  107.0 9.3 %copy-start.34 = (bf16[1,1024,1024]{2,1,0:T(8,128)(2,1)S(1)}, bf16[1,1024,1024]{2,1,0:T(8,128)(2,1)}, u32[]{:S(2)}) copy-start(bf16[1,1024,1024]{2,1,0:T(8,128)(2,1)} %param.13) | copy-start | bytes 6291460
  107.0 9.3 %copy-start.52 = (bf16[2048,1024]{1,0:T(8,128)(2,1)S(1)}, bf16[2048,1024]{1,0:T(8,128)(2,1)}, u32[]{:S(2)}) copy-start(bf16[2048,1024]{1,0:T(8,128)(2,1)} %param.21) | copy-start | bytes 12582916
  129.4 2.0 copy-start.33
  137.5 376.3 %all-reduce.9.cloned.1.call-start = ((), (), s32[]{:S(2)}) async-start(), calls=%async_computation.2 | async-start | bytes 16777216 | tf_op jit(solution)/shard_map/psum | solution.py:310
  167.2 15.3 %copy-start.10 = (f32[1024,1024]{1,0:T(8,128)S(1)}, f32[1024,1024]{1,0:T(8,128)}, u32[]{:S(2)}) copy-start(f32[1024,1024]{1,0:T(8,128)} %all-reduce.7.cloned.1.call-done) | copy-start | bytes 12582916
  182.5 2.2 copy-start.4
  184.7 5.7 slice-start
  184.7 6.0 %slice-start.1 = ((s8[16777216]{0:T(1024)(128)(4,1)}), s8[4194304]{0:T(1024)(128)(4,1)S(1)}, s32[]{:S(2)}) async-start(s8[16777216]{0:T(1024)(128)(4,1)} %bitcast.217), calls=%async_computation.4 | async-start | bytes 8388608
  184.7 8.1 %slice-start.2 = ((s8[16777216]{0:T(1024)(128)(4,1)}), s8[4194304]{0:T(1024)(128)(4,1)S(1)}, s32[]{:S(2)}) async-start(s8[16777216]{0:T(1024)(128)(4,1)} %bitcast.217), calls=%async_computation.5 | async-start | bytes 8388608
  188.3 2.1 copy-start.13
  188.3 5.7 slice-start.3
  190.4 15.5 %copy-start.24 = (bf16[1024,512]{0,1:T(8,128)(2,1)}, bf16[1024,512]{0,1:T(8,128)(2,1)S(1)}, u32[]{:S(2)}) copy-start(bf16[1024,512]{0,1:T(8,128)(2,1)S(1)} %fusion.58) | copy-start | bytes 3145732
  193.9 4.0 copy-start.28
  216.9 15.3 %copy-start.15 = (bf16[1,1024,8,32]{1,3,2,0:T(8,128)(2,1)S(1)}, bf16[1,1024,8,32]{1,3,2,0:T(8,128)(2,1)}, u32[]{:S(2)}) copy-start(bf16[1,1024,8,32]{1,3,2,0:T(8,128)(2,1)} %copy-done.14) | copy-start | bytes 1572868
  216.9 15.3 %copy-start.17 = (bf16[1,1024,8,32]{1,3,2,0:T(8,128)(2,1)S(1)}, bf16[1,1024,8,32]{1,3,2,0:T(8,128)(2,1)}, u32[]{:S(2)}) copy-start(bf16[1,1024,8,32]{1,3,2,0:T(8,128)(2,1)} %copy-done.16) | copy-start | bytes 1572868
  228.9 3.3 copy-start.7
  232.2 2.9 copy-start.19
  232.2 2.9 copy-start.21
  235.1 7.2 %copy-start.23 = (f32[8,64,1024]{2,1,0:T(8,128)S(1)}, f32[8,64,1024]{2,1,0:T(8,128)}, u32[]{:S(2)}) copy-start(f32[8,64,1024]{2,1,0:T(8,128)} %fusion.10) | copy-start | bytes 6291460
  235.1 7.2 %copy-start.25 = (bf16[1024,512]{0,1:T(8,128)(2,1)S(1)}, bf16[1024,512]{0,1:T(8,128)(2,1)}, u32[]{:S(2)}) copy-start(bf16[1024,512]{0,1:T(8,128)(2,1)} %copy-done.24) | copy-start | bytes 3145732
  261.3 6.2 %copy-start.6 = (bf16[8,512,1024]{2,1,0:T(8,128)(2,1)S(1)}, bf16[8,512,1024]{2,1,0:T(8,128)(2,1)}, u32[]{:S(2)}) copy-start(bf16[8,512,1024]{2,1,0:T(8,128)(2,1)} %multiply_convert_fusion) | copy-start | bytes 25165828
  261.3 6.4 %copy-start.12 = (f32[8,64,1024]{2,1,0:T(8,128)S(1)}, f32[8,64,1024]{2,1,0:T(8,128)}, u32[]{:S(2)}) copy-start(f32[8,64,1024]{2,1,0:T(8,128)} %fusion.90) | copy-start | bytes 6291460
  267.6 1.6 copy-start.29
  267.6 1.6 copy-start.36
  267.6 1.6 copy-start.38
  269.2 1.2 copy-start.41
  270.1 1.7 copy-start.30
  270.5 1.4 copy-start.42
  271.9 1.4 copy-start.31
  271.9 1.6 copy-start.22
  271.9 1.9 copy-start.40
  277.1 1.6 copy-start.9
  277.1 1.6 copy-start.46
  277.1 1.6 copy-start.48
  277.1 1.6 copy-start.50
  297.3 8.2 %copy-start.32 = (bf16[1024,512]{1,0:T(8,128)(2,1)S(1)}, bf16[1024,512]{1,0:T(8,128)(2,1)}, u32[]{:S(2)}) copy-start(bf16[1024,512]{1,0:T(8,128)(2,1)} %copy.73) | copy-start | bytes 3145732
  513.7 3.5 copy-start.11
  513.7 44.4 %copy-start.5 = (f32[1,1024,1024]{2,1,0:T(8,128)S(1)}, f32[1,1024,1024]{2,1,0:T(8,128)}, u32[]{:S(2)}) copy-start(f32[1,1024,1024]{2,1,0:T(8,128)} %copy-done.3) | copy-start | bytes 12582916
  558.2 6.4 %copy-start.1 = (bf16[512,1024]{1,0:T(8,128)(2,1)S(1)}, bf16[512,1024]{1,0:T(8,128)(2,1)}, u32[]{:S(2)}) copy-start(bf16[512,1024]{1,0:T(8,128)(2,1)} %param.19) | copy-start | bytes 3145732
Sparse Core Ops, SparseCore 0:
  69.2 31.1 all-reduce.4
  137.6 29.5 all-reduce.6
  277.3 40.0 all-reduce.8
